TPU v7x, 256 devices: a whole 4x4x8 slice. The times are simulated.
256 devices in a mesh: chan: 8 (over x_lo, y), ctx: 32 (over x_hi, z, core).
Axes of the slice: x: 4 (x_hi: 2, x_lo: 2; x = x_hi * 2 + x_lo), y: 4, z: 8, core: 2. Of those that a mesh axis runs over, the one named last changes fastest.
Arguments:
- inputs: bfloat16 [4096, 8192], P('ctx', 'chan'), may hold values from -6 to 6
- w_value: bfloat16 [8192, 4096], P('ctx', 'chan'), may hold values from -0.125 to 0.125
- q_field: bfloat16 [4096, 4096], P('ctx', 'chan'), may hold values from -6 to 6
- k_field: bfloat16 [4096, 4096], P('ctx', 'chan'), may hold values from -6 to 6
- filters: float32 [128, 4096], P(None, 'chan'), may hold values from -1.2 to 1.2
- out_grad: bfloat16 [4096, 4096], P('ctx', 'chan'), may hold values from -6 to 6
Outputs:
- in_grad: bfloat16 [4096, 8192], P('ctx', 'chan')
- w_grad: bfloat16 [8192, 4096], P('ctx', 'chan')
- q_grad: bfloat16 [4096, 4096], P('ctx', 'chan')
- k_grad: bfloat16 [4096, 4096], P('ctx', 'chan')
- filter_grad: float32 [128, 4096], P(None, 'chan')
All inputs are finite; a program needn't handle non-finite values.
Results may differ from a plain program's by a relative error of at most 0.033.
Values may be sent and summed in bfloat16 or wider, within the bound.
A program may use at most 64 MiB of HBM per device.

v0:
```python
import jax
import jax.numpy as jnp
from jax import lax
from jax.sharding import PartitionSpec as P


def from_behind(shard, axis, by):
    count = lax.axis_size(axis)
    pairs = [(i, i + by) for i in range(count) if 0 <= i + by < count]
    return lax.ppermute(shard, axis, pairs)


def tap_sums(filters, fwd_ext, bwd_ext, grad_h32, rows):
    taps = filters.shape[0]
    width = taps - 1
    group = 8
    chans = filters.shape[1]

    def step_fn(block_index, carry):
        forward, adjoint, filter_part = carry
        rows_part = []
        for offset in range(group):
            tap = block_index * group + offset
            coeff = lax.dynamic_slice_in_dim(filters, tap, 1, 0)
            shifted = lax.dynamic_slice_in_dim(fwd_ext, width - tap, rows, 0)
            ahead = lax.dynamic_slice_in_dim(bwd_ext, tap, rows, 0)
            forward = forward + coeff * shifted
            adjoint = adjoint + coeff * ahead
            rows_part.append(jnp.sum(grad_h32 * shifted, axis=0, keepdims=True))
        filter_part = lax.dynamic_update_slice_in_dim(
            filter_part, jnp.concatenate(rows_part, 0), block_index * group, 0
        )
        return (forward, adjoint, filter_part)

    start = (
        jnp.zeros((rows, chans), jnp.float32),
        jnp.zeros((rows, chans), jnp.float32),
        jnp.zeros((taps, chans), jnp.float32),
    )
    return lax.fori_loop(0, taps // group, step_fn, start)


def body(inputs, w_value, q_field, k_field, filters, out_grad):
    rows = inputs.shape[0]
    width = filters.shape[0] - 1
    full_rows = lax.all_gather(inputs, "chan", axis=1, tiled=True)
    w_full = lax.all_gather(w_value, "ctx", axis=0, tiled=True)
    value_acc = jnp.dot(full_rows, w_full, preferred_element_type=jnp.float32)
    values = value_acc.astype(jnp.bfloat16)
    gated = (k_field.astype(jnp.float32) * values.astype(jnp.float32)).astype(jnp.bfloat16)
    grad_h = (out_grad.astype(jnp.float32) * q_field.astype(jnp.float32)).astype(jnp.bfloat16)
    field_rim = from_behind(gated[rows - width :], "ctx", 1)
    grad_rim = from_behind(grad_h[:width], "ctx", -1)
    fwd_ext = jnp.concatenate([field_rim, gated], 0).astype(jnp.float32)
    grad_h32 = grad_h.astype(jnp.float32)
    bwd_ext = jnp.concatenate([grad_h32, grad_rim.astype(jnp.float32)], 0)
    filtered, grad_g, filter_local = tap_sums(filters, fwd_ext, bwd_ext, grad_h32, rows)
    filter_grad = lax.psum(filter_local.astype(jnp.bfloat16), "ctx").astype(jnp.float32)
    q_grad = (out_grad.astype(jnp.float32) * filtered).astype(jnp.bfloat16)
    k_grad = (grad_g * values.astype(jnp.float32)).astype(jnp.bfloat16)
    v_grad = (grad_g * k_field.astype(jnp.float32)).astype(jnp.bfloat16)
    w_grad = lax.psum_scatter(
        lax.dot_general(
            full_rows, v_grad, (((0,), (0,)), ((), ())), preferred_element_type=jnp.float32
        ).astype(jnp.bfloat16),
        "ctx",
        scatter_dimension=0,
        tiled=True,
    )
    in_sum = lax.psum_scatter(
        lax.dot_general(
            w_full, v_grad, (((1,), (1,)), ((), ())), preferred_element_type=jnp.float32
        ).astype(jnp.bfloat16),
        "chan",
        scatter_dimension=0,
        tiled=True,
    ).astype(jnp.float32)
    in_grad = in_sum.T.astype(jnp.bfloat16)
    return (in_grad, w_grad, q_grad, k_grad, filter_grad)


def solution(mesh):
    return jax.shard_map(
        body,
        mesh=mesh,
        in_specs=(
            P("ctx", "chan"),
            P("ctx", "chan"),
            P("ctx", "chan"),
            P("ctx", "chan"),
            P(None, "chan"),
            P("ctx", "chan"),
        ),
        out_specs=(
            P("ctx", "chan"),
            P("ctx", "chan"),
            P("ctx", "chan"),
            P("ctx", "chan"),
            P(None, "chan"),
        ),
        check_vma=False,
    )
```

profile of v0, /device:TPU:1, one launch (start us, length us, event | category | flops | bytes accessed | tf_op | source)
XLA Modules:
  0.0 748.1 jit_solution(6235177519943005645)
XLA Ops:
  9.7 5.1 collective-permute-start.1
  14.9 37.6 %all-gather.3.cloned.1.call-done = bf16[128,8192]{1,0:T(8,128)(2,1)} async-done(((bf16[128,1024]{1,0:T(8,128)(2,1)}), bf16[128,8192]{1,0:T(8,128)(2,1)}) %all-gather.3.cloned.1.call-update) | async-done | bytes 2097168 | tf_op jit(solution)/shard_map/all_gather | solution.py:46
  52.5 109.2 %all-gather.5.cloned.1.call-done = bf16[8192,512]{1,0:T(8,128)(2,1)} async-done(((bf16[256,512]{1,0:T(8,128)(2,1)}), bf16[8192,512]{1,0:T(8,128)(2,1)}) %all-gather.5.cloned.1.call-update) | async-done | bytes 8388624 | tf_op jit(solution)/shard_map/all_gather | solution.py:47
  161.7 5.9 fusion.17
  167.7 3.0 collective-permute-start
  173.3 128.5 %while.21 = (s32[]{:T(128)}, f32[128,512]{1,0:T(8,128)}, f32[128,512]{1,0:T(8,128)S(1)}, bf16[128,512]{1,0:T(8,128)(2,1)}, f32[128,512]{1,0:T(8,128)}, /*index=5...) while((s32[]{:T(128)}, f32[128,512]{1,0:T(8,128)}, ...), condition=%wide.region_9.0_spmd.clone, body=%wide.region_0.0_spmd.clone.sunk | while | flops 3272787 | bytes 7726444 | solution.py:40
  175.0 1.9 multiply_reduce_fusion.9
  186.0 2.0 fusion.31
  190.8 1.9 multiply_reduce_fusion.9
  194.1 2.0 fusion.31
  202.1 2.0 fusion.31
  210.2 2.0 fusion.31
  218.2 2.0 fusion.31
  226.3 2.0 fusion.31
  231.1 1.9 multiply_reduce_fusion.9
  234.3 2.0 fusion.31
  239.2 1.9 multiply_reduce_fusion.9
  242.4 2.0 fusion.31
  250.5 2.0 fusion.31
  258.5 2.0 fusion.31
  266.6 2.0 fusion.31
  274.6 2.0 fusion.31
  282.7 2.0 fusion.31
  287.5 1.9 multiply_reduce_fusion.9
  290.8 2.0 fusion.31
  295.6 1.9 multiply_reduce_fusion.9
  298.8 2.0 fusion.31
  302.0 5.6 fusion.14
  307.7 7.6 %fusion.15 = bf16[8192,128]{0,1:T(8,128)(2,1)} fusion(bf16[8192,512]{1,0:T(8,128)(2,1)} %all-gather.5.cloned.1.call-done, f32[128,512]{1,0:T(8,128)S(1)} %get-tuple-element.275, bf16[128,512]{1,0:T(8,128)(2,1)S(1)} %copy-done.3), kind=kOutput, calls=%fused_computation.36 | convolution fusion | flops 1074987008 | bytes 10878976 | tf_op jit(solution)/shard_map/dot_general | solution.py:71
  316.1 227.4 %all-reduce.2.cloned.1.call-done = bf16[128,512]{1,0:T(8,128)(2,1)} async-done(((bf16[128,512]{1,0:T(8,128)(2,1)}), bf16[128,512]{1,0:T(8,128)(2,1)}) %all-reduce.2.cloned.1.call-update) | async-done | bytes 131088 | tf_op jit(solution)/shard_map/psum | solution.py:58
  545.1 150.6 %reduce-scatter.5.cloned.1.call-done = bf16[256,512]{0,1:T(8,128)(2,1)} async-done(((bf16[8192,512]{0,1:T(8,128)(2,1)}), bf16[256,512]{0,1:T(8,128)(2,1)}) %reduce-scatter.5.cloned.1.call-update) | async-done | bytes 262160 | tf_op jit(solution)/shard_map/reduce_scatter | solution.py:62
  697.5 44.0 %reduce-scatter.3.cloned.1.call-done = bf16[1024,128]{0,1:T(8,128)(2,1)} async-done(((bf16[8192,128]{0,1:T(8,128)(2,1)}), bf16[1024,128]{0,1:T(8,128)(2,1)}) %reduce-scatter.3.cloned.1.call-update) | async-done | bytes 262160 | tf_op jit(solution)/shard_map/reduce_scatter | solution.py:70
  (110 shorter events, 94.7 us)
Async XLA Ops:
  7.2 45.3 %all-gather.3.cloned.1.call-start = ((), (), s32[]{:S(2)}) async-start(), calls=%async_computation.2 | async-start | bytes 2359296 | tf_op jit(solution)/shard_map/all_gather | solution.py:46
  7.9 153.8 %all-gather.5.cloned.1.call-start = ((), (), s32[]{:S(2)}) async-start(), calls=%async_computation.3 | async-start | bytes 8650752 | tf_op jit(solution)/shard_map/all_gather | solution.py:47
  8.6 534.9 %all-reduce.2.cloned.1.call-start = ((), (), s32[]{:S(2)}) async-start(), calls=%async_computation.6 | async-start | bytes 262144 | tf_op jit(solution)/shard_map/psum | solution.py:58
  9.7 161.0 %copy-start.1 = (f32[128,512]{1,0:T(8,128)}, f32[128,512]{1,0:T(8,128)S(1)}, u32[]{:S(2)}) copy-start(f32[128,512]{1,0:T(8,128)S(1)} %get-tuple-element.436) | copy-start | bytes 786436
  9.7 161.0 %collective-permute-start.1 = (bf16[127,512]{1,0:T(8,128)(2,1)S(1)}, bf16[127,512]{1,0:T(8,128)(2,1)S(1)}, u32[]{:S(2)}, u32[]{:S(2)}) collective-permute-start(bf16[127,512]{1,0:T(8,128)(2,1)S(1)} %bitcast.82), channel_id=1, source_target_pairs={{1,0},{2,1},{3,2},{4,3},{5,4},{6,5},{7,6},{8,7},{9,8},{10,9},{11,1... | collective-permute-start | bytes 390152 | tf_op jit(solution)/shard_map/ppermute | solution.py:10
  167.7 4.9 collective-permute-start
  173.3 128.6 %copy-start = (bf16[128,8192]{1,0:T(8,128)(2,1)S(1)}, bf16[128,8192]{1,0:T(8,128)(2,1)}, u32[]{:S(2)}) copy-start(bf16[128,8192]{1,0:T(8,128)(2,1)} %all-gather.3.cloned.1.call-done) | copy-start | bytes 6291460
  173.3 128.6 %copy-start.3 = (bf16[128,512]{1,0:T(8,128)(2,1)S(1)}, bf16[128,512]{1,0:T(8,128)(2,1)}, u32[]{:S(2)}) copy-start(bf16[128,512]{1,0:T(8,128)(2,1)} %param.11) | copy-start | bytes 393220
  301.9 393.8 %reduce-scatter.5.cloned.1.call-start = ((), (), s32[]{:S(2)}) async-start(), calls=%async_computation.5 | async-start | bytes 8650752 | tf_op jit(solution)/shard_map/reduce_scatter | solution.py:62
  307.6 7.7 %copy-start.2 = (f32[128,512]{1,0:T(8,128)S(1)}, f32[128,512]{1,0:T(8,128)}, u32[]{:S(2)}) copy-start(f32[128,512]{1,0:T(8,128)} %get-tuple-element.276) | copy-start | bytes 786436
  307.6 7.7 %copy-start.4 = (f32[128,512]{1,0:T(8,128)S(1)}, f32[128,512]{1,0:T(8,128)}, u32[]{:S(2)}) copy-start(f32[128,512]{1,0:T(8,128)} %get-tuple-element.345) | copy-start | bytes 786436
  307.6 7.7 %copy-start.5 = (bf16[128,512]{1,0:T(8,128)(2,1)S(1)}, bf16[128,512]{1,0:T(8,128)(2,1)}, u32[]{:S(2)}) copy-start(bf16[128,512]{1,0:T(8,128)(2,1)} %param.13) | copy-start | bytes 393220
  307.6 433.9 %reduce-scatter.3.cloned.1.call-start = ((), (), s32[]{:S(2)}) async-start(), calls=%async_computation.4 | async-start | bytes 2359296 | tf_op jit(solution)/shard_map/reduce_scatter | solution.py:70
Sparse Core Ops, SparseCore 0:
  9.8 42.6 all-gather.2
  55.2 106.4 all-gather.4
  302.0 241.4 all-reduce.1
  548.4 147.3 reduce-scatter.4
  698.9 42.6 reduce-scatter.2
where the time goes:
time: 755 us; the launch traced here: 748 us
  waiting for transfers between devices  572 us (76%)
  other arithmetic  82.3 us (11%)
  local copies, waits for them, and re-layouts  50.3 us (7%)
  matrix products  19.1 us (3%)
  between operations  13.9 us (2%)
  starting transfers between devices  8.35 us (1%)
    psum x1, waiting for transfers between devices, body(): lax.psum(filter_local.astype(jnp.bfloat16), 'ctx').astype(jnp.float32)  227 us
    reduce_scatter x1, waiting for transfers between devices, body(): lax.psum_scatter(lax.dot_general(full_rows, v_grad, (((0,), (0,)), ((), (...  151 us
    all_gather x1, waiting for transfers between devices, body(): w_full = lax.all_gather(w_value, 'ctx', axis=0, tiled=True)  109 us
    reduce_scatter x1, waiting for transfers between devices, body(): lax.psum_scatter(lax.dot_general(w_full, v_grad, (((1,), (1,)), ((), ()))...  44 us
    all_gather x1, waiting for transfers between devices, body(): full_rows = lax.all_gather(inputs, 'chan', axis=1, tiled=True)  37.6 us
    add x16, other arithmetic, step_fn(): forward = forward + coeff * shifted  31.7 us
    reduce_sum x16, other arithmetic, step_fn(): rows_part.append(jnp.sum(grad_h32 * shifted, axis=0, keepdims=True))  30.4 us
    dynamic_slice x16, local copies, waits for them, and re-layouts, step_fn(): coeff = lax.dynamic_slice_in_dim(filters, tap, 1, 0)  26.3 us
  transfers between devices with their start and end apart: 7, of which 6 were waited for; matrix products, arithmetic and copies ran while one was open for 3% of the time, Pallas kernels for 0%

commit v1 on v0

v1 whole, which is shorter than its diff:
```python
import jax
import jax.numpy as jnp
import ml_dtypes
import numpy as np
from jax import lax
from jax.experimental import pallas as pl
from jax.experimental.pallas import tpu as pltpu
from jax.sharding import PartitionSpec as P

MESH = pl.DeviceIdType.MESH
F32, BF16 = jnp.float32, jnp.bfloat16
BLK = 128
CH = 512
NX, NY, NZ = 2, 4, 8
N_CTX = 2 * NZ * 2

R_IN1, R_IN2, R_W, R_WX = 0, 8, 11, 25
R_H, R_G, R_V, R_VC, R_VX = 26, 27, 28, 35, 39
R_RS, R_IG1, R_IG2, R_WG = 42, 56, 59, 67
R_F1, R_F2, R_F3, R_F4 = 68, 71, 78, 85
N_RECV = 88
N_SEND = 110
N_LOCAL = 16


def transforms():
    k, n = np.arange(BLK)[:, None], np.arange(BLK)[None, :]
    angle = np.pi * (2 * k + 1) * n / (2 * BLK)
    full = np.concatenate([np.cos(angle), -np.sin(angle)], 0)
    high = full.astype(ml_dtypes.bfloat16)
    low = (full - high.astype(np.float64)).astype(ml_dtypes.bfloat16)
    forward = np.concatenate([high, low], 0)
    inverse = np.concatenate([high.T, low.T], 0).astype(np.float32) / BLK
    return forward, inverse.astype(ml_dtypes.bfloat16)


def kernel(
    x_hbm, w_hbm, q_hbm, k_hbm, f_hbm, o_hbm, fwd_hbm, inv_hbm,
    ig_hbm, wg_hbm, qg_hbm, kg_hbm, fg_hbm,
    q_v, k_v, o_v, f_v, fwd_v, inv_v,
    h_v, hn_v, g_v, gp_v, fs_v, hs_v, gg_v,
    gin, wfull, vfull,
    rs_out, rs_in,
    val_t, val_s, val_c, val_xs, val_xr,
    ig_s, ig_r, ig_sum,
    qg_v, kg_v, fq_s, fq_r, fz_s, fz_r, fz_all, fq_all, fg_v,
    wg_own, wg_par,
    ssem, rsem, lsem,
):
    chan, ctx = lax.axis_index("chan"), lax.axis_index("ctx")
    xl, y = chan // NY, chan % NY
    xh, z, core = ctx // (2 * NZ), (ctx // 2) % NZ, ctx % 2
    tb = xh * 2 + core
    xo = 1 - xl

    def dev(xh_, xl_, y_, z_, core_):
        return (xl_ * NY + y_, xh_ * (2 * NZ) + z_ * 2 + core_)

    def plane(d):
        return dev((xh + d // 4) % 2, (xl + (d // 2) % 2) % 2, y, z, (core + d % 2) % 2)

    def y_peer(d):
        return dev(xh, xl, (y + d) % NY, z, core)

    def z_peer(d):
        return dev(xh, xl, y, (z + d + NZ) % NZ, core)

    def ctx_peer(d):
        return (chan, (ctx + d + N_CTX) % N_CTX)

    right, left, partner = z_peer(1), z_peer(-1), plane(2)
    started = []
    local_ids = iter(range(N_LOCAL))

    def send(src, dst, device, recv):
        copy = pltpu.make_async_remote_copy(
            src_ref=src, dst_ref=dst, send_sem=ssem.at[len(started)], recv_sem=rsem.at[recv],
            device_id=device, device_id_type=MESH,
        )
        copy.start()
        started.append(copy)

    def arrive(dst, recv):
        pltpu.make_async_copy(dst, dst, rsem.at[recv]).wait()

    def local(src, dst):
        copy = pltpu.make_async_copy(src, dst, lsem.at[next(local_ids)])
        copy.start()
        return copy

    def rows(index, size=BLK):
        return pl.ds(pl.multiple_of(index * size, size), size)

    def dot(a, b):
        return jnp.dot(a, b, preferred_element_type=F32)

    loads = [local(a, b) for a, b in (
        (o_hbm, o_v), (q_hbm, q_v), (fwd_hbm, fwd_v), (f_hbm, f_v), (inv_hbm, inv_v), (k_hbm, k_v))]
    w_local = local(w_hbm.at[rows(xl), :], wfull.at[xl, rows(z), :])
    barrier = pltpu.get_barrier_semaphore()
    greeted = [plane(d) for d in range(1, 8)] + [y_peer(d) for d in range(1, NY)]
    greeted += [z_peer(d) for d in range(1, NZ)] + [ctx_peer(1), ctx_peer(-1)]
    for device in greeted:
        pl.semaphore_signal(barrier, inc=1, device_id=device, device_id_type=MESH)
    pl.semaphore_wait(barrier, len(greeted))

    def w_piece(half, zz):
        return wfull.at[half, rows(zz), :]

    send(w_hbm.at[rows(xl), :], w_piece(xl, z), right, R_W + 0)
    send(w_hbm.at[rows(xl), :], w_piece(xl, z), left, R_W + 7)
    send(w_hbm.at[rows(xo), :], w_piece(xl, z), partner, R_WX)

    def in_slab(b9, xl_, core_):
        return pl.ds(pl.multiple_of(b9 * 512 + core_ * 256 + xl_ * 128, 128), 128)

    def gin_slab(b9):
        return gin.at[rows(tb), pl.ds(pl.multiple_of(y * 256 + b9 * 128, 128), 128)]

    self_sends = []
    for a in range(2):
        for b in range(2):
            xl_d, core_d = (xl + a) % 2, (core + b) % 2
            for b9 in range(2):
                src = x_hbm.at[:, in_slab(b9, xl_d, core_d)]
                if a == 0 and b == 0:
                    far = pltpu.make_async_remote_copy(
                        src_ref=src, dst_ref=gin_slab(b9), send_sem=ssem.at[N_SEND - 1 - b9],
                        recv_sem=rsem.at[R_IN1 + tb * 2 + b9],
                        device_id=dev(xl, xl_d, y, z, core_d), device_id_type=MESH,
                    )
                    near = pltpu.make_async_copy(src, gin_slab(b9), rsem.at[R_IN1 + tb * 2 + b9])

                    @pl.when(xh != xl)
                    def _():
                        far.start()

                    @pl.when(xh == xl)
                    def _():
                        near.start()

                    self_sends.append(far)
                else:
                    send(src, gin_slab(b9), dev(xl, xl_d, y, z, core_d), R_IN1 + tb * 2 + b9)

    loads[0].wait()
    loads[1].wait()
    h = (o_v[...].astype(F32) * q_v[...].astype(F32)).astype(BF16)
    h_v[...] = h
    send(h_v, hn_v, ctx_peer(-1), R_H)

    def forward(block):
        t = dot(fwd_v[...], block)
        return t[:256] + t[256:]

    def inverse(re, im):
        spec = jnp.concatenate([re, im], 0)
        high = spec.astype(BF16)
        low = (spec - high.astype(F32)).astype(BF16)
        t = dot(inv_v[...], high)
        return t[:BLK] + t[BLK:] + dot(inv_v[:BLK], low)

    sign = (1 - 2 * (lax.broadcasted_iota(jnp.int32, (BLK, CH), 0) % 2)).astype(F32)
    loads[2].wait()
    loads[3].wait()
    taps = f_v[...]
    taps_high = taps.astype(BF16)
    taps_low = (taps - taps_high.astype(F32)).astype(BF16)
    fs_v[...] = forward(taps_high) + dot(fwd_v[:256], taps_low)
    hs_v[...] = forward(h)

    w_local.wait()
    arrive(w_piece(xo, z), R_WX)
    send(w_piece(xo, z), w_piece(xo, z), right, R_W + 1)
    send(w_piece(xo, z), w_piece(xo, z), left, R_W + 8)

    def w_from_left(i, forward_on=True):
        half = xl if i % 2 == 0 else xo
        piece = w_piece(half, (z - (i // 2 + 1) + NZ) % NZ)
        arrive(piece, R_W + i)
        if i < 5:
            send(piece, piece, right, R_W + i + 2)

    def w_from_right(i):
        half = xo if i % 2 == 1 or i == 6 else xl
        piece = w_piece(half, (z + (i // 2 + 1)) % NZ)
        arrive(piece, R_W + 7 + i)
        if i < 4:
            send(piece, piece, left, R_W + 7 + i + 2)
        elif i == 5:
            send(piece, piece, left, R_W + 7 + 6)

    w_from_left(0)
    w_from_right(0)

    for i in range(4):
        for b9 in range(2):
            arrive(gin.at[rows(i), pl.ds(pl.multiple_of(y * 256 + b9 * 128, 128), 128)], R_IN1 + i * 2 + b9)

    def gin_cols(yy):
        return gin.at[:, pl.ds(pl.multiple_of(yy * 256, 256), 256)]

    for d in range(1, NY):
        send(gin_cols(y), gin_cols(y), y_peer(d), R_IN2 + d - 1)

    arrive(hn_v, R_H)
    last = ctx == N_CTX - 1
    loads[4].wait()
    loads[5].wait()
    hn = forward(jnp.where(last, jnp.zeros_like(h), hn_v[...]))
    hr = hs_v[:BLK] + sign * hn[BLK:]
    hi = hs_v[BLK:] - sign * hn[:BLK]
    fr, fi = fs_v[:BLK], fs_v[BLK:]
    g_grad = inverse(fr * hr + fi * hi, fr * hi - fi * hr)
    gg_v[...] = g_grad
    mine = vfull.at[xl, rows(tb), :]
    vfull[xl, rows(tb), :] = (g_grad * k_v[...].astype(F32)).astype(BF16)
    for d in (4, 6, 2, 5, 7, 3, 1):
        send(mine, mine, plane(d), R_V + d - 1)

    for i in range(1, 3):
        w_from_left(i)
        w_from_right(i)

    for d in range(1, 8):
        xh_s, xl_s, core_s = (xh + d // 4) % 2, (xl + (d // 2) % 2) % 2, (core + d % 2) % 2
        arrive(vfull.at[xl_s, rows(xh_s * 2 + core_s), :], R_V + d - 1)
    for d in range(1, NY):
        arrive(gin_cols((y - d + NY) % NY), R_IN2 + d - 1)

    def w_term(zz, half):
        part = gin[:, pl.ds(pl.multiple_of(zz * 128, 128), 128)]
        return lax.dot_general(part, vfull[half], (((0,), (0,)), ((), ())), preferred_element_type=F32)

    def rs_step(i):
        hop = 4 - (i + 1) // 2
        for way, device, step in ((0, right, 1), (1, left, -1)):
            half = xl if (i + way) % 2 == 0 else xo
            term = w_term((z + step * hop + NZ) % NZ, half)
            if i >= 2:
                arrive(rs_in.at[way, i - 2], R_RS + way * 7 + i - 2)
                term = term + rs_in[way, i - 2].astype(F32)
            rs_out[way, i] = term.astype(BF16)
            send(rs_out.at[way, i], rs_in.at[way, i], device, R_RS + way * 7 + i)

    rs_step(0)
    rs_step(1)
    for i in range(3, 6):
        w_from_left(i)
        w_from_right(i)
    w_from_left(6)
    w_from_right(6)

    for j in (1, 2, 3, 0):
        xh_d, xl_d = (xh + j // 2) % 2, (xl + j % 2) % 2
        val_t[j] = dot(gin[rows(xh_d, 256), :], wfull[xl_d])
        val_s[j] = val_t[j, rows(1 - core), :].astype(BF16)
        send(val_s.at[j], val_c.at[j], plane(1), R_VC + j)
    rs_step(2)
    for j in (1, 2, 3):
        arrive(val_c.at[j], R_VC + j)
        val_xs[j - 1] = (val_t[j, rows(core), :] + val_c[j].astype(F32)).astype(BF16)
        send(val_xs.at[j - 1], val_xr.at[j - 1], plane(2 * j), R_VX + j - 1)

    def in_term(yy):
        total = 0.0
        for half in range(2):
            total = total + lax.dot_general(
                vfull[half], wfull[half, rows(yy, 256), :], (((1,), (1,)), ((), ())), preferred_element_type=F32
            )
        return total

    for d in (2, 1, 3):
        ig_s[d - 1] = in_term((y + d) % NY).astype(BF16)
        send(ig_s.at[d - 1], ig_r.at[d - 1], y_peer(d), R_IG1 + d - 1)
    rs_step(3)

    arrive(val_c.at[0], R_VC)
    value = val_t[0, rows(core), :] + val_c[0].astype(F32)
    for j in range(3):
        arrive(val_xr.at[j], R_VX + j)
        value = value + val_xr[j].astype(F32)
    value = value.astype(BF16).astype(F32)
    gated = (k_v[...].astype(F32) * value).astype(BF16)
    g_v[...] = gated
    send(g_v, gp_v, ctx_peer(1), R_G)
    kg_v[...] = (gg_v[...] * value).astype(BF16)
    outs = [local(kg_v, kg_hbm)]
    own = forward(gated)
    rs_step(4)
    ig_own = in_term(y)
    arrive(gp_v, R_G)
    before = forward(jnp.where(ctx == 0, jnp.zeros_like(gated), gp_v[...]))
    er = own[:BLK] - sign * before[BLK:]
    ei = own[BLK:] + sign * before[:BLK]
    hr, hi = hs_v[:BLK], hs_v[BLK:]
    filter_part = inverse(hr * er + hi * ei, hi * er - hr * ei)

    quarter = [filter_part[:, i * 128 : (i + 1) * 128] for i in range(4)]
    for i in range(4):
        fg_v[:, i * 128 : (i + 1) * 128] = quarter[i]
        fq_s[i] = quarter[i].astype(BF16)
    group = ((1, 1), (2, 4), (3, 5))
    for place, d in group:
        xh_d, core_d = (xh + d // 4) % 2, (core + d % 2) % 2
        send(fq_s.at[xh_d * 2 + core_d], fq_r.at[place - 1], plane(d), R_F1 + place - 1)
    fr, fi = fs_v[:BLK], fs_v[BLK:]
    filtered = inverse(fr * er - fi * ei, fr * ei + fi * er)
    qg_v[...] = (o_v[...].astype(F32) * filtered).astype(BF16)
    outs.append(local(qg_v, qg_hbm))
    rs_step(5)

    total = fg_v[:, pl.ds(pl.multiple_of(tb * 128, 128), 128)]
    for place in range(3):
        arrive(fq_r.at[place], R_F1 + place)
        total = total + fq_r[place].astype(F32)
    fg_v[:, :128] = total
    for i in range(NZ):
        fz_s[i] = total[i * 16 : (i + 1) * 16].astype(BF16)
    for d in range(1, NZ):
        send(fz_s.at[(z + d) % NZ], fz_r.at[d - 1], z_peer(d), R_F2 + d - 1)

    for d in range(1, NY):
        arrive(ig_r.at[d - 1], R_IG1 + d - 1)
        ig_own = ig_own + ig_r[d - 1].astype(F32)
    ig_sum[...] = ig_own.astype(BF16)
    for a in range(2):
        for b in range(2):
            xh_d, core_d = (xh + a) % 2, (core + b) % 2
            for b9 in range(2):
                src = ig_sum.at[rows(xh_d * 2 + core_d), b9 * 128 : (b9 + 1) * 128]
                dst = ig_hbm.at[:, in_slab(b9, xl, core)]
                recv = R_IG2 + (xl * 2 + core) * 2 + b9
                if a == 0 and b == 0:
                    far = pltpu.make_async_remote_copy(
                        src_ref=src, dst_ref=dst, send_sem=ssem.at[N_SEND - 3 - b9], recv_sem=rsem.at[recv],
                        device_id=dev(xh_d, xh, y, z, core_d), device_id_type=MESH,
                    )
                    near = pltpu.make_async_copy(src, dst, rsem.at[recv])

                    @pl.when(xh != xl)
                    def _():
                        far.start()

                    @pl.when(xh == xl)
                    def _():
                        near.start()

                    self_sends.append(far)
                else:
                    send(src, dst, dev(xh_d, xh, y, z, core_d), recv)

    rs_step(6)

    piece = fg_v[rows(z, 16), :128]
    for d in range(1, NZ):
        arrive(fz_r.at[d - 1], R_F2 + d - 1)
        piece = piece + fz_r[d - 1].astype(F32)
    fz_all[z] = piece.astype(BF16)
    for d in range(1, NZ):
        send(fz_all.at[z], fz_all.at[z], z_peer(d), R_F3 + d - 1)

    def w_total(half, first, second):
        arrive(rs_in.at[0, first], R_RS + first)
        arrive(rs_in.at[1, second], R_RS + 7 + second)
        total = w_term(z, half) + rs_in[0, first].astype(F32) + rs_in[1, second].astype(F32)
        return total.astype(BF16)

    wg_par[...] = w_total(xo, 5, 6)
    send(wg_par, wg_hbm.at[rows(xl), :], partner, R_WG)
    wg_own[...] = w_total(xl, 6, 5)
    outs.append(local(wg_own, wg_hbm.at[rows(xl), :]))

    for d in range(1, NZ):
        arrive(fz_all.at[(z - d + NZ) % NZ], R_F3 + d - 1)
    for i in range(NZ):
        fq_all[tb, i * 16 : (i + 1) * 16, :] = fz_all[i]
    for place, d in group:
        send(fq_all.at[tb], fq_all.at[tb], plane(d), R_F4 + place - 1)
    for place, d in group:
        xh_s, core_s = (xh + d // 4) % 2, (core + d % 2) % 2
        arrive(fq_all.at[xh_s * 2 + core_s], R_F4 + place - 1)
    for i in range(4):
        fg_v[:, i * 128 : (i + 1) * 128] = fq_all[i].astype(F32)
    outs.append(local(fg_v, fg_hbm))

    for xl_s in range(2):
        for core_s in range(2):
            for b9 in range(2):
                arrive(ig_hbm.at[:, in_slab(b9, xl_s, core_s)], R_IG2 + (xl_s * 2 + core_s) * 2 + b9)
    arrive(wg_hbm.at[rows(xo), :], R_WG)
    for copy in started:
        copy.wait_send()

    @pl.when(xh != xl)
    def _():
        for copy in self_sends:
            copy.wait_send()

    for copy in outs:
        copy.wait()


def body(inputs, w_value, q_field, k_field, filters, out_grad):
    forward, inverse = transforms()
    blk = (BLK, CH)
    vmem = pltpu.VMEM
    scratch = [
        vmem(blk, BF16), vmem(blk, BF16), vmem(blk, BF16), vmem(blk, F32),
        vmem((512, BLK), BF16), vmem((256, 256), BF16),
        vmem(blk, BF16), vmem(blk, BF16), vmem(blk, BF16), vmem(blk, BF16),
        vmem((256, CH), F32), vmem((256, CH), F32), vmem(blk, F32),
        vmem((512, 1024), BF16), vmem((2, 1024, CH), BF16), vmem((2, 512, CH), BF16),
        vmem((2, 7) + blk, BF16), vmem((2, 7) + blk, BF16),
        vmem((4, 256, CH), F32), vmem((4,) + blk, BF16), vmem((4,) + blk, BF16),
        vmem((3,) + blk, BF16), vmem((3,) + blk, BF16),
        vmem((3, 512, 256), BF16), vmem((3, 512, 256), BF16), vmem((512, 256), BF16),
        vmem(blk, BF16), vmem(blk, BF16),
        vmem((4, BLK, 128), BF16), vmem((3, BLK, 128), BF16),
        vmem((NZ, 16, 128), BF16), vmem((NZ - 1, 16, 128), BF16), vmem((NZ, 16, 128), BF16),
        vmem((4, BLK, 128), BF16), vmem(blk, F32),
        vmem(blk, BF16), vmem(blk, BF16),
        pltpu.SemaphoreType.DMA((N_SEND,)),
        pltpu.SemaphoreType.DMA((N_RECV,)),
        pltpu.SemaphoreType.DMA((N_LOCAL,)),
    ]
    any_space = pl.BlockSpec(memory_space=pl.ANY)
    return pl.pallas_call(
        kernel,
        out_shape=(
            jax.ShapeDtypeStruct((BLK, 1024), BF16),
            jax.ShapeDtypeStruct((256, CH), BF16),
            jax.ShapeDtypeStruct(blk, BF16),
            jax.ShapeDtypeStruct(blk, BF16),
            jax.ShapeDtypeStruct(blk, F32),
        ),
        in_specs=[any_space] * 8,
        out_specs=[any_space] * 5,
        scratch_shapes=scratch,
        compiler_params=pltpu.CompilerParams(
            collective_id=0, has_side_effects=True, vmem_limit_bytes=48 * 1024 * 1024
        ),
        cost_estimate=pl.CostEstimate(flops=4 * 2**30, bytes_accessed=4 * 2**20, transcendentals=0),
    )(inputs, w_value, q_field, k_field, filters, out_grad, jnp.asarray(forward), jnp.asarray(inverse))


def solution(mesh):
    return jax.shard_map(
        body,
        mesh=mesh,
        in_specs=(
            P("ctx", "chan"),
            P("ctx", "chan"),
            P("ctx", "chan"),
            P("ctx", "chan"),
            P(None, "chan"),
            P("ctx", "chan"),
        ),
        out_specs=(
            P("ctx", "chan"),
            P("ctx", "chan"),
            P("ctx", "chan"),
            P("ctx", "chan"),
            P(None, "chan"),
        ),
        check_vma=False,
    )
```

time: 755 us -> 97.1 us (0.13)
  waiting for transfers between devices: 572 us -> 0 us
  Pallas kernels: 0 us -> 85.4 us
  other arithmetic: 82.3 us -> 0 us
  local copies, waits for them, and re-layouts: 50.3 us -> 10.8 us
  matrix products: 19.1 us -> 0 us
  between operations: 13.9 us -> 0.66 us
  starting transfers between devices: 8.35 us -> 0 us
    psum x1 -> x0, waiting for transfers between devices: 227 us -> none  [body(): lax.psum(filter_local.astype(jnp.bfloat16), 'ctx').astype(jnp.float32)]
    reduce_scatter x2 -> x0, waiting for transfers between devices: 195 us -> none  [the longest x1 151 us: body(): lax.psum_scatter(lax.dot_general(full_rows, v_grad, (((0,), (0,)), ((), (...]
    all_gather x2 -> x0, waiting for transfers between devices: 147 us -> none  [the longest x1 109 us: body(): w_full = lax.all_gather(w_value, 'ctx', axis=0, tiled=True)]
    pallas_call x0 -> x1, Pallas kernels: none -> 85.4 us  [body(): pl.pallas_call(kernel, out_shape=(jax.ShapeDtypeStruct((BLK, 1024), BF16)...]
    add x32 -> x0, other arithmetic: 48.4 us -> none  [the longest x16 31.7 us: step_fn(): forward = forward + coeff * shifted]
    reduce_sum x16 -> x0, other arithmetic: 30.4 us -> none  [step_fn(): rows_part.append(jnp.sum(grad_h32 * shifted, axis=0, keepdims=True))]
    dynamic_slice x16 -> x0, local copies, waits for them, and re-layouts: 26.3 us -> none  [step_fn(): coeff = lax.dynamic_slice_in_dim(filters, tap, 1, 0)]
    dot_general x3 -> x0, matrix products: 19.1 us -> none  [the longest x1 7.6 us: body(): lax.dot_general(w_full, v_grad, (((1,), (1,)), ((), ())), preferred_eleme...]
  transfers between devices with their start and end apart: 7 -> 0, of which waited for: 6 -> 0; matrix products, arithmetic and copies ran while one was open for 3% -> 0% of each run, Pallas kernels for 0% -> 0%
where the time goes in v1:
time: 97.1 us; the launch traced here: 96.8 us
  Pallas kernels  85.4 us (88%)
  local copies, waits for them, and re-layouts  10.8 us (11%)
    pallas_call x1, Pallas kernels, body(): pl.pallas_call(kernel, out_shape=(jax.ShapeDtypeStruct((BLK, 1024), BF16)...  85.4 us
    unnamed x21, local copies, waits for them, and re-layouts  10.8 us

profile of v1, /device:TPU:1, one launch (start us, length us, event | category | flops | bytes accessed | tf_op | source)
XLA Modules:
  0.0 96.8 jit_solution(17704523779893273577)
XLA Ops:
  0.6 0.0 copy-start
  0.6 0.9 copy-done
  1.6 0.0 copy-start.1
  1.6 0.9 copy-done.1
  2.5 0.0 copy-start.2
  2.5 0.9 copy-done.2
  3.5 0.0 copy-start.3
  3.5 0.9 copy-done.3
  4.4 0.0 copy-start.4
  4.4 0.9 copy-done.4
  5.3 0.0 copy-start.5
  5.3 0.9 copy-done.5
  6.2 0.0 copy-start.6
  6.2 0.9 copy-done.6
  7.1 0.0 copy-start.7
  7.1 0.9 copy-done.7
  8.0 85.4 %shard_map.119 = (bf16[128,1024]{1,0:T(8,128)(2,1)S(1)}, bf16[256,512]{1,0:T(8,128)(2,1)S(1)}, bf16[128,512]{1,0:T(8,128)(2,1)S(1)}, bf16[128,512]{1,0:T(8,128)(2,1)S(1)}, f32[128,512]{1,0:T(8,128)S(1)}) custom-call(bf16[128,1024]{1,0:T(8,128)(2,1)S(1)} %copy-done, bf16[256,512]{1,0:T(8,128)(2,1)S(1)} %copy-done.1, bf16[128,512]{1,0:T(8,128)(2,1)S(1)} %copy-done.3, ...), custom_call_target="tpu_custom_call" | custom-call | flops 4294967296 | bytes 4194304 | tf_op jit(solution)/shard_map/pallas_call | solution.py:428
  93.4 0.7 copy.18
  94.1 0.7 copy.19
  94.8 0.7 copy.20
  95.5 0.7 copy.21
  96.1 0.7 copy.22
Async XLA Ops:
  0.6 1.0 copy-start
  1.6 0.9 copy-start.1
  2.5 0.9 copy-start.2
  3.5 0.9 copy-start.3
  4.4 0.9 copy-start.4
  5.3 0.9 copy-start.5
  6.2 0.9 copy-start.6
  7.1 0.9 copy-start.7

commit v2 on v1

v2 whole, which is shorter than its diff:
```python
import jax
import jax.numpy as jnp
import ml_dtypes
import numpy as np
from jax import lax
from jax.experimental import pallas as pl
from jax.experimental.pallas import tpu as pltpu
from jax.sharding import PartitionSpec as P

MESH = pl.DeviceIdType.MESH
F32, BF16 = jnp.float32, jnp.bfloat16
BLK = 128
CH = 512
NX, NY, NZ = 2, 4, 8
N_CTX = 2 * NZ * 2

R_IN1, R_IN2, R_WX, R_WRO, R_WRP, R_WLO, R_WLP = 0, 8, 14, 15, 19, 22, 25
R_H, R_G, R_V, R_VC, R_VX = 29, 30, 31, 38, 42
R_RS, R_RSX, R_WG, R_IG1, R_IG2 = 45, 59, 61, 62, 68
R_F1, R_F2, R_F3, R_F4 = 76, 79, 86, 93
N_RECV = 96
N_SEND = 120
N_LOCAL = 16
VMEM_LIMIT = 60 * 1024 * 1024


def transforms():
    k, n = np.arange(BLK)[:, None], np.arange(BLK)[None, :]
    angle = np.pi * (2 * k + 1) * n / (2 * BLK)
    full = np.concatenate([np.cos(angle), -np.sin(angle)], 0)
    high = full.astype(ml_dtypes.bfloat16)
    low = (full - high.astype(np.float64)).astype(ml_dtypes.bfloat16)
    forward = np.concatenate([high, low], 0)
    inverse = np.concatenate([high.T, low.T], 0).astype(np.float32) / BLK
    halves = np.concatenate([inverse[:, :BLK], inverse[:, BLK:]], 0)
    return forward, halves.astype(ml_dtypes.bfloat16)


def kernel(
    x_hbm, w_hbm, q_hbm, k_hbm, f_hbm, o_hbm, fwd_hbm, inv_hbm,
    ig_hbm, wg_hbm, qg_hbm, kg_hbm, fg_hbm,
    q_v, k_v, o_v, f_v, fwd_v, inv_v,
    h_v, hn_v, g_v, gp_v, fs_v, hs_v, gg_v,
    gin, wfull, vfull,
    rs_out, rs_in, rs_x, wx_s, wx_r,
    val_t, val_s, val_c, val_xs, val_xr,
    ig_s, ig_r, ig_sum,
    qg_v, kg_v, fq_s, fq_r, fz_s, fz_r, fz_all, fq_all, fg_v,
    wg_v,
    ssem, rsem, lsem,
):
    chan, ctx = lax.axis_index("chan"), lax.axis_index("ctx")
    xl, y = chan // NY, chan % NY
    xh, z, core = ctx // (2 * NZ), (ctx // 2) % NZ, ctx % 2
    tb = xh * 2 + core
    xo = 1 - xl

    def dev(xh_, xl_, y_, z_, core_):
        return (xl_ * NY + y_, xh_ * (2 * NZ) + z_ * 2 + core_)

    def bits(d):
        return (xh + d // 4) % 2, (xl + (d // 2) % 2) % 2, (core + d % 2) % 2

    def plane(d):
        xh_, xl_, core_ = bits(d)
        return dev(xh_, xl_, y, z, core_)

    def y_peer(d):
        return dev(xh, xl, (y + d) % NY, z, core)

    def z_peer(d):
        return dev(xh, xl, y, (z + d + NZ) % NZ, core)

    def z_partner(d):
        return dev(xh, xo, y, (z + d + NZ) % NZ, core)

    def ctx_peer(d):
        return (chan, (ctx + d + N_CTX) % N_CTX)

    right, left, partner, sibling = z_peer(1), z_peer(-1), plane(2), plane(1)
    started = []
    local_ids = iter(range(N_LOCAL))

    def send(src, dst, device, recv):
        copy = pltpu.make_async_remote_copy(
            src_ref=src, dst_ref=dst, send_sem=ssem.at[len(started)], recv_sem=rsem.at[recv],
            device_id=device, device_id_type=MESH,
        )
        copy.start()
        started.append(copy)

    def arrive(dst, recv):
        pltpu.make_async_copy(dst, dst, rsem.at[recv]).wait()

    def local(src, dst):
        copy = pltpu.make_async_copy(src, dst, lsem.at[next(local_ids)])
        copy.start()
        return copy

    def rows(index, size=BLK):
        return pl.ds(pl.multiple_of(index * size, size), size)

    def lanes(index, size=128):
        return pl.ds(pl.multiple_of(index * size, size), size)

    def dot(a, b):
        return jnp.dot(a, b, preferred_element_type=F32)

    def forward(block):
        t = dot(fwd_v[...], block)
        return t[:256] + t[256:]

    def inverse(re, im):
        spec = jnp.concatenate([re, im], 0)
        high = spec.astype(BF16)
        low = (spec - high.astype(F32)).astype(BF16)
        t = dot(inv_v[...], high)
        return t[:BLK] + t[BLK:] + dot(inv_v[:BLK], low)

    sign = (1 - 2 * (lax.broadcasted_iota(jnp.int32, (BLK, CH), 0) % 2)).astype(F32)

    loads = [local(a, b) for a, b in (
        (o_hbm, o_v), (q_hbm, q_v), (fwd_hbm, fwd_v), (f_hbm, f_v), (k_hbm, k_v),
        (inv_hbm.at[:256], inv_v.at[:, :BLK]), (inv_hbm.at[256:], inv_v.at[:, BLK:]))]
    w_local = local(w_hbm.at[rows(xl), :], wfull.at[xl, rows(z), :])
    barrier = pltpu.get_barrier_semaphore()
    greeted = [plane(d) for d in range(1, 8)] + [y_peer(d) for d in range(1, NY)]
    greeted += [z_peer(d) for d in range(1, NZ)] + [ctx_peer(1), ctx_peer(-1), z_partner(1), z_partner(-1)]
    for device in greeted:
        pl.semaphore_signal(barrier, inc=1, device_id=device, device_id_type=MESH)
    loads[0].wait()
    loads[1].wait()
    h = (o_v[...].astype(F32) * q_v[...].astype(F32)).astype(BF16)
    h_v[...] = h
    loads[2].wait()
    loads[3].wait()
    taps = f_v[...]
    taps_high = taps.astype(BF16)
    taps_low = (taps - taps_high.astype(F32)).astype(BF16)
    fs_v[...] = forward(taps_high) + dot(fwd_v[:256], taps_low)
    hs_v[...] = forward(h)
    pl.semaphore_wait(barrier, len(greeted))

    def w_piece(half, zz):
        return wfull.at[half, rows(zz), :]

    send(w_hbm.at[rows(xl), :], w_piece(xl, z), right, R_WRO)
    send(w_hbm.at[rows(xl), :], w_piece(xl, z), left, R_WLO)
    send(w_hbm.at[rows(xo), :], w_piece(xl, z), partner, R_WX)
    send(h_v, hn_v, ctx_peer(-1), R_H)

    def in_slab(b9, xl_, core_):
        return lanes(b9 * 4 + core_ * 2 + xl_)

    def gin_slab(place, b9):
        return gin.at[rows(place), lanes(y * 2 + b9)]

    self_sends = []

    def send_or_copy(src, dst, device, recv, same_x):
        if not same_x:
            return send(src, dst, device, recv)
        far = pltpu.make_async_remote_copy(
            src_ref=src, dst_ref=dst, send_sem=ssem.at[N_SEND - 1 - len(self_sends)], recv_sem=rsem.at[recv],
            device_id=device, device_id_type=MESH,
        )
        near = pltpu.make_async_copy(src, dst, rsem.at[recv])
        self_sends.append(far)

        @pl.when(xh != xl)
        def _():
            far.start()

        @pl.when(xh == xl)
        def _():
            near.start()

    for a in (1, 0):
        for b in (1, 0):
            xl_d, core_d = (xl + a) % 2, (core + b) % 2
            for b9 in range(2):
                src = x_hbm.at[:, in_slab(b9, xl_d, core_d)]
                send_or_copy(src, gin_slab(tb, b9), dev(xl, xl_d, y, z, core_d), R_IN1 + tb * 2 + b9, a + b == 0)

    def gin_part(place, yy):
        return gin.at[rows(place, 256), lanes(yy, 256)]

    def in_second(turn):
        place = (xl + turn) % 2
        for i in range(2):
            for b9 in range(2):
                arrive(gin_slab(place * 2 + i, b9), R_IN1 + (place * 2 + i) * 2 + b9)
        for d in (2, 1, 3):
            send(gin_part(place, y), gin_part(place, y), y_peer(d), R_IN2 + (d - 1) * 2 + place)

    def w_own(k):
        piece = w_piece(xl, (z - k + NZ) % NZ)
        arrive(piece, R_WRO + k - 1)
        if k < 4:
            send(piece, piece, right, R_WRO + k)
            piece = w_piece(xl, (z + k) % NZ)
            arrive(piece, R_WLO + k - 1)
            if k < 3:
                send(piece, piece, left, R_WLO + k)

    def w_par(k):
        piece = w_piece(xo, (z + k) % NZ)
        arrive(piece, R_WLP + k - 1)
        if k < 4:
            send(piece, piece, left, R_WLP + k)
            piece = w_piece(xo, (z - k + NZ) % NZ)
            arrive(piece, R_WRP + k - 1)
            if k < 3:
                send(piece, piece, right, R_WRP + k)

    w_local.wait()
    w_own(1)
    arrive(w_piece(xo, z), R_WX)
    send(w_piece(xo, z), w_piece(xo, z), left, R_WLP)
    send(w_piece(xo, z), w_piece(xo, z), right, R_WRP)
    in_second(0)

    arrive(hn_v, R_H)
    for load in loads[4:]:
        load.wait()
    hn = forward(jnp.where(ctx == N_CTX - 1, jnp.zeros_like(h), hn_v[...]))
    hr = hs_v[:BLK] + sign * hn[BLK:]
    hi = hs_v[BLK:] - sign * hn[:BLK]
    hs_v[:BLK] = hr
    hs_v[BLK:] = hi
    fr, fi = fs_v[:BLK], fs_v[BLK:]
    g_grad = inverse(fr * hr + fi * hi, fr * hi - fi * hr)
    gg_v[...] = g_grad
    vfull[xl, rows(tb), :] = (g_grad * k_v[...].astype(F32)).astype(BF16)

    def v_piece(d):
        xh_, xl_, core_ = bits(d)
        return vfull.at[xl_, rows(xh_ * 2 + core_), :]

    for d in (4, 6, 2, 1):
        send(v_piece(0), v_piece(0), plane(d), R_V + d - 1)
    in_second(1)
    w_own(2)
    w_par(1)
    w_own(3)
    w_par(2)
    for d in (2, 6, 4):
        arrive(v_piece(d), R_V + d - 1)
        send(v_piece(d), v_piece(d), sibling, R_V + d)
    w_own(4)
    w_par(3)
    for d in (1, 3, 5, 7):
        arrive(v_piece(d), R_V + d - 1)
    for place in range(2):
        for d in range(1, NY):
            arrive(gin_part(place, (y - d + NY) % NY), R_IN2 + (d - 1) * 2 + place)

    def w_term(zz, half):
        return lax.dot_general(
            gin[:, lanes(zz)], vfull[half], (((0,), (0,)), ((), ())), preferred_element_type=F32
        )

    def rs_step(i):
        hop = 4 - (i + 1) // 2
        for way, step in ((0, 1), (1, -1)):
            own = (i + way) % 2 == 0
            term = w_term((z + step * hop + NZ) % NZ, xl if own else xo)
            if i >= 2:
                arrive(rs_in.at[way, i - 2], R_RS + way * 7 + i - 2)
                term = term + rs_in[way, i - 2].astype(F32)
            rs_out[way, i] = term.astype(BF16)
            if hop == 1 and not own:
                send(rs_out.at[way, i], rs_x.at[way], z_partner(step), R_RSX + way)
            else:
                send(rs_out.at[way, i], rs_in.at[way, i], z_peer(step), R_RS + way * 7 + i)

    rs_step(0)
    rs_step(1)

    def val_part(j):
        xh_d, xl_d, _ = bits(2 * j)
        val_t[j] = dot(gin[rows(xh_d, 256), :], wfull[xl_d])
        val_s[j] = val_t[j, rows(1 - core), :].astype(BF16)
        send(val_s.at[j], val_c.at[j], sibling, R_VC + j)

    def val_send(j):
        arrive(val_c.at[j], R_VC + j)
        val_xs[j - 1] = (val_t[j, rows(core), :] + val_c[j].astype(F32)).astype(BF16)
        send(val_xs.at[j - 1], val_xr.at[j - 1], plane(2 * j), R_VX + j - 1)

    val_part(2)
    val_part(0)
    val_send(2)
    w_par(4)
    val_part(1)
    val_part(3)
    val_send(1)
    val_send(3)
    rs_step(2)

    def in_term(place, yy):
        total = 0.0
        for half in range(2):
            total = total + lax.dot_general(
                vfull[half, rows(place, 256), :], wfull[half, rows(yy, 256), :], (((1,), (1,)), ((), ())),
                preferred_element_type=F32,
            )
        return total

    def ig_first(turn):
        place = (xo + turn) % 2
        for d in (2, 1, 3):
            slot = (d - 1) * 2 + turn
            ig_s[slot] = in_term(place, (y + d) % NY).astype(BF16)
            send(ig_s.at[slot], ig_r.at[slot], y_peer(d), R_IG1 + slot)

    def ig_second(turn):
        place = (xo + turn) % 2
        total = in_term(place, y)
        for d in (1, 3, 2):
            slot = (d - 1) * 2 + turn
            arrive(ig_r.at[slot], R_IG1 + slot)
            total = total + ig_r[slot].astype(F32)
        ig_sum[turn] = total.astype(BF16)
        for b in (1, 0):
            core_d = (core + b) % 2
            for b9 in range(2):
                src = ig_sum.at[turn, rows(core_d), b9 * 128 : (b9 + 1) * 128]
                dst = ig_hbm.at[:, in_slab(b9, xl, core)]
                send_or_copy(src, dst, dev(place, xh, y, z, core_d), R_IG2 + (xl * 2 + core) * 2 + b9, turn + b == 1 and b == 0)

    ig_first(0)
    ig_first(1)
    rs_step(3)
    wx_s[...] = w_term(z, xo).astype(BF16)
    send(wx_s, wx_r, partner, R_WG)

    arrive(val_c.at[0], R_VC)
    value = val_t[0, rows(core), :] + val_c[0].astype(F32)
    for j in (2, 1, 3):
        arrive(val_xr.at[j - 1], R_VX + j - 1)
        value = value + val_xr[j - 1].astype(F32)
    value = value.astype(BF16).astype(F32)
    gated = (k_v[...].astype(F32) * value).astype(BF16)
    g_v[...] = gated
    send(g_v, gp_v, ctx_peer(1), R_G)
    own = forward(gated)
    hr, hi = hs_v[:BLK], hs_v[BLK:]
    filter_part = inverse(own[:BLK] * hr + own[BLK:] * hi, own[:BLK] * hi - own[BLK:] * hr)
    fg_v[...] = filter_part

    for i in range(4):
        fq_s[i] = filter_part[:, i * 128 : (i + 1) * 128].astype(BF16)
    group = ((1, 1), (2, 4), (3, 5))
    for place, d in group:
        xh_d, _, core_d = bits(d)
        send(fq_s.at[xh_d * 2 + core_d], fq_r.at[place - 1], plane(d), R_F1 + place - 1)
    kg_v[...] = (gg_v[...] * value).astype(BF16)
    outs = [local(kg_v, kg_hbm)]
    rs_step(4)

    total = fg_v[:, lanes(tb)]
    for place in range(3):
        arrive(fq_r.at[place], R_F1 + place)
        total = total + fq_r[place].astype(F32)
    fg_v[:, :128] = total
    for i in range(NZ):
        fz_s[i] = total[i * 16 : (i + 1) * 16].astype(BF16)
    for d in range(1, NZ):
        send(fz_s.at[(z + d) % NZ], fz_r.at[d - 1], z_peer(d), R_F2 + d - 1)
    rs_step(5)
    ig_second(0)

    arrive(gp_v, R_G)
    before = forward(jnp.where(ctx == 0, jnp.zeros_like(gated), gp_v[...]))
    er = own[:BLK] - sign * before[BLK:]
    ei = own[BLK:] + sign * before[:BLK]
    fr, fi = fs_v[:BLK], fs_v[BLK:]
    filtered = inverse(fr * er - fi * ei, fr * ei + fi * er)
    qg_v[...] = (o_v[...].astype(F32) * filtered).astype(BF16)
    outs.append(local(qg_v, qg_hbm))

    piece = fg_v[rows(z, 16), :128]
    for d in range(1, NZ):
        arrive(fz_r.at[d - 1], R_F2 + d - 1)
        piece = piece + fz_r[d - 1].astype(F32)
    fz_all[z] = piece.astype(BF16)
    for d in range(1, NZ):
        send(fz_all.at[z], fz_all.at[z], z_peer(d), R_F3 + d - 1)
    rs_step(6)
    ig_second(1)

    for d in range(1, NZ):
        arrive(fz_all.at[(z - d + NZ) % NZ], R_F3 + d - 1)
    for i in range(NZ):
        fq_all[tb, i * 16 : (i + 1) * 16, :] = fz_all[i]
    for place, d in group:
        send(fq_all.at[tb], fq_all.at[tb], plane(d), R_F4 + place - 1)

    term = w_term(z, xl)
    arrive(rs_in.at[1, 5], R_RS + 7 + 5)
    term = term + rs_in[1, 5].astype(F32)
    arrive(wx_r, R_WG)
    arrive(rs_x.at[0], R_RSX)
    other = wx_r[...].astype(F32) + rs_x[0].astype(F32)
    arrive(rs_in.at[0, 6], R_RS + 6)
    wg_v[0] = (term + rs_in[0, 6].astype(F32)).astype(BF16)
    outs.append(local(wg_v.at[0], wg_hbm.at[rows(xl), :]))
    arrive(rs_x.at[1], R_RSX + 1)
    wg_v[1] = (other + rs_x[1].astype(F32)).astype(BF16)
    outs.append(local(wg_v.at[1], wg_hbm.at[rows(xo), :]))

    for place, d in group:
        xh_s, _, core_s = bits(d)
        arrive(fq_all.at[xh_s * 2 + core_s], R_F4 + place - 1)
    for i in range(4):
        fg_v[:, i * 128 : (i + 1) * 128] = fq_all[i].astype(F32)
    outs.append(local(fg_v, fg_hbm))

    for xl_s in range(2):
        for core_s in range(2):
            for b9 in range(2):
                arrive(ig_hbm.at[:, in_slab(b9, xl_s, core_s)], R_IG2 + (xl_s * 2 + core_s) * 2 + b9)
    for copy in started:
        copy.wait_send()

    @pl.when(xh != xl)
    def _():
        for copy in self_sends:
            copy.wait_send()

    for copy in outs:
        copy.wait()


def copy_kernel(*refs):
    sources, targets, sem = refs[:5], refs[5:10], refs[10]
    copies = [pltpu.make_async_copy(a, b, sem.at[i]) for i, (a, b) in enumerate(zip(sources, targets))]
    for copy in copies:
        copy.start()
    for copy in copies:
        copy.wait()


def body(inputs, w_value, q_field, k_field, filters, out_grad):
    forward, inverse = transforms()
    blk = (BLK, CH)
    vmem = pltpu.VMEM
    scratch = [
        vmem(blk, BF16), vmem(blk, BF16), vmem(blk, BF16), vmem(blk, F32),
        vmem((512, BLK), BF16), vmem((256, 256), BF16),
        vmem(blk, BF16), vmem(blk, BF16), vmem(blk, BF16), vmem(blk, BF16),
        vmem((256, CH), F32), vmem((256, CH), F32), vmem(blk, F32),
        vmem((512, 1024), BF16), vmem((2, 1024, CH), BF16), vmem((2, 512, CH), BF16),
        vmem((2, 7) + blk, BF16), vmem((2, 7) + blk, BF16), vmem((2,) + blk, BF16),
        vmem(blk, BF16), vmem(blk, BF16),
        vmem((4, 256, CH), F32), vmem((4,) + blk, BF16), vmem((4,) + blk, BF16),
        vmem((3,) + blk, BF16), vmem((3,) + blk, BF16),
        vmem((6, 256, 256), BF16), vmem((6, 256, 256), BF16), vmem((2, 256, 256), BF16),
        vmem(blk, BF16), vmem(blk, BF16),
        vmem((4, BLK, 128), BF16), vmem((3, BLK, 128), BF16),
        vmem((NZ, 16, 128), BF16), vmem((NZ - 1, 16, 128), BF16), vmem((NZ, 16, 128), BF16),
        vmem((4, BLK, 128), BF16), vmem(blk, F32),
        vmem((2,) + blk, BF16),
        pltpu.SemaphoreType.DMA((N_SEND,)),
        pltpu.SemaphoreType.DMA((N_RECV,)),
        pltpu.SemaphoreType.DMA((N_LOCAL,)),
    ]
    any_space = pl.BlockSpec(memory_space=pl.ANY)
    hbm_space = pl.BlockSpec(memory_space=pltpu.HBM)
    shapes = (
        jax.ShapeDtypeStruct((BLK, 1024), BF16),
        jax.ShapeDtypeStruct((256, CH), BF16),
        jax.ShapeDtypeStruct(blk, BF16),
        jax.ShapeDtypeStruct(blk, BF16),
        jax.ShapeDtypeStruct(blk, F32),
    )
    results = pl.pallas_call(
        kernel,
        out_shape=tuple(vmem(s.shape, s.dtype) for s in shapes),
        in_specs=[hbm_space] * 8,
        out_specs=[any_space] * 5,
        scratch_shapes=scratch,
        compiler_params=pltpu.CompilerParams(
            collective_id=0, has_side_effects=True, vmem_limit_bytes=VMEM_LIMIT
        ),
        cost_estimate=pl.CostEstimate(flops=4 * 2**30, bytes_accessed=4 * 2**20, transcendentals=0),
    )(inputs, w_value, q_field, k_field, filters, out_grad, jnp.asarray(forward), jnp.asarray(inverse))
    return pl.pallas_call(
        copy_kernel,
        out_shape=shapes,
        in_specs=[any_space] * 5,
        out_specs=[hbm_space] * 5,
        scratch_shapes=[pltpu.SemaphoreType.DMA((5,))],
        compiler_params=pltpu.CompilerParams(vmem_limit_bytes=8 * 1024 * 1024),
    )(*results)


def solution(mesh):
    return jax.shard_map(
        body,
        mesh=mesh,
        in_specs=(
            P("ctx", "chan"),
            P("ctx", "chan"),
            P("ctx", "chan"),
            P("ctx", "chan"),
            P(None, "chan"),
            P("ctx", "chan"),
        ),
        out_specs=(
            P("ctx", "chan"),
            P("ctx", "chan"),
            P("ctx", "chan"),
            P("ctx", "chan"),
            P(None, "chan"),
        ),
        check_vma=False,
    )
```

time: 97.1 us -> 68.3 us (0.70)
  Pallas kernels: 85.4 us -> 67.6 us
  local copies, waits for them, and re-layouts: 10.8 us -> 0 us
    pallas_call x1 -> x2, Pallas kernels: 85.4 us -> 67.6 us  [the longest x1 66.6 us: body(): pl.pallas_call(kernel, out_shape=tuple((vmem(s.shape, s.dtype) for s in s...]
    unnamed x21 -> x0, local copies, waits for them, and re-layouts: 10.8 us -> none
where the time goes in v2:
time: 68.3 us; the launch traced here: 68.2 us
  Pallas kernels  67.6 us (99%)
    pallas_call x1, Pallas kernels, body(): pl.pallas_call(kernel, out_shape=tuple((vmem(s.shape, s.dtype) for s in s...  66.6 us

profile of v2, /device:TPU:1, one launch (start us, length us, event | category | flops | bytes accessed | tf_op | source)
XLA Modules:
  0.0 68.2 jit_solution(15557438594265057947)
XLA Ops:
  0.6 66.6 %shard_map.119 = (bf16[128,1024]{1,0:T(8,128)(2,1)S(1)}, bf16[256,512]{1,0:T(8,128)(2,1)S(1)}, bf16[128,512]{1,0:T(8,128)(2,1)S(1)}, bf16[128,512]{1,0:T(8,128)(2,1)S(1)}, f32[128,512]{1,0:T(8,128)S(1)}) custom-call(bf16[128,1024]{1,0:T(8,128)(2,1)} %x_hbm.1, bf16[256,512]{1,0:T(8,128)(2,1)} %w_hbm.1, bf16[128,512]{1,0:T(8,128)(2,1)} %q_hbm.1, ...), custom_call_target="tpu_custom_call" | custom-call | flops 4294967296 | bytes 4194304 | tf_op jit(solution)/shard_map/pallas_call | solution.py:478
  67.2 1.0 %shard_map.120 = (bf16[128,1024]{1,0:T(8,128)(2,1)}, bf16[256,512]{1,0:T(8,128)(2,1)}, bf16[128,512]{1,0:T(8,128)(2,1)}, bf16[128,512]{1,0:T(8,128)(2,1)}, f32[128,512]{1,0:T(8,128)}) custom-call(bf16[128,1024]{1,0:T(8,128)(2,1)S(1)} %get-tuple-element.10.refs_0_, bf16[256,512]{1,0:T(8,128)(2,1)S(1)} %get-tuple-element.11.refs_1_, ...), custom_call_target="tpu_custom_call" | custom-call | tf_op jit(solution)/shard_map/pallas_call | solution.py:489

commit v3 on v2

--- a/solution.py
+++ b/solution.py
@@ -14,12 +14,12 @@
 NX, NY, NZ = 2, 4, 8
 N_CTX = 2 * NZ * 2
 
-R_IN1, R_IN2, R_WX, R_WRO, R_WRP, R_WLO, R_WLP = 0, 8, 14, 15, 19, 22, 25
-R_H, R_G, R_V, R_VC, R_VX = 29, 30, 31, 38, 42
-R_RS, R_RSX, R_WG, R_IG1, R_IG2 = 45, 59, 61, 62, 68
-R_F1, R_F2, R_F3, R_F4 = 76, 79, 86, 93
-N_RECV = 96
-N_SEND = 120
+R_IN1, R_IN2, R_WX, R_WR, R_WL = 0, 8, 14, 16, 32
+R_H, R_G, R_V, R_VC, R_VX = 48, 49, 50, 57, 61
+R_RS, R_RSX, R_WG, R_IG1, R_IG2 = 64, 78, 80, 81, 87
+R_F1, R_F2, R_F3, R_F4 = 95, 98, 105, 112
+N_RECV = 115
+N_SEND = 140
 N_LOCAL = 16
 VMEM_LIMIT = 60 * 1024 * 1024
 
@@ -128,26 +128,19 @@
     greeted += [z_peer(d) for d in range(1, NZ)] + [ctx_peer(1), ctx_peer(-1), z_partner(1), z_partner(-1)]
     for device in greeted:
         pl.semaphore_signal(barrier, inc=1, device_id=device, device_id_type=MESH)
-    loads[0].wait()
-    loads[1].wait()
-    h = (o_v[...].astype(F32) * q_v[...].astype(F32)).astype(BF16)
-    h_v[...] = h
-    loads[2].wait()
-    loads[3].wait()
-    taps = f_v[...]
-    taps_high = taps.astype(BF16)
-    taps_low = (taps - taps_high.astype(F32)).astype(BF16)
-    fs_v[...] = forward(taps_high) + dot(fwd_v[:256], taps_low)
-    hs_v[...] = forward(h)
     pl.semaphore_wait(barrier, len(greeted))
 
-    def w_piece(half, zz):
-        return wfull.at[half, rows(zz), :]
-
-    send(w_hbm.at[rows(xl), :], w_piece(xl, z), right, R_WRO)
-    send(w_hbm.at[rows(xl), :], w_piece(xl, z), left, R_WLO)
-    send(w_hbm.at[rows(xo), :], w_piece(xl, z), partner, R_WX)
-    send(h_v, hn_v, ctx_peer(-1), R_H)
+    def w_piece(stream, zz):
+        return wfull.at[xl if stream < 2 else xo, rows(zz * 2 + stream % 2, 64), :]
+
+    def w_start(stream, src):
+        send(src, w_piece(stream, z), right, R_WR + stream * 4)
+        send(src, w_piece(stream, z), left, R_WL + stream * 4)
+
+    for part in range(2):
+        send(w_hbm.at[rows(xo * 2 + part, 64), :], w_piece(part, z), partner, R_WX + part)
+    for part in range(2):
+        w_start(part, w_hbm.at[rows(xl * 2 + part, 64), :])
 
     def in_slab(b9, xl_, core_):
         return lanes(b9 * 4 + core_ * 2 + xl_)
@@ -182,6 +175,19 @@
                 src = x_hbm.at[:, in_slab(b9, xl_d, core_d)]
                 send_or_copy(src, gin_slab(tb, b9), dev(xl, xl_d, y, z, core_d), R_IN1 + tb * 2 + b9, a + b == 0)
 
+    loads[0].wait()
+    loads[1].wait()
+    h = (o_v[...].astype(F32) * q_v[...].astype(F32)).astype(BF16)
+    h_v[...] = h
+    send(h_v, hn_v, ctx_peer(-1), R_H)
+    loads[2].wait()
+    loads[3].wait()
+    taps = f_v[...]
+    taps_high = taps.astype(BF16)
+    taps_low = (taps - taps_high.astype(F32)).astype(BF16)
+    fs_v[...] = forward(taps_high) + dot(fwd_v[:256], taps_low)
+    hs_v[...] = forward(h)
+
     def gin_part(place, yy):
         return gin.at[rows(place, 256), lanes(yy, 256)]
 
@@ -193,31 +199,28 @@
         for d in (2, 1, 3):
             send(gin_part(place, y), gin_part(place, y), y_peer(d), R_IN2 + (d - 1) * 2 + place)
 
+    def w_step(stream, k):
+        for step, base, hops in ((1, R_WR, 4 - stream % 2), (-1, R_WL, 3 + stream % 2)):
+            if k > hops:
+                continue
+            piece = w_piece(stream, (z - step * k + NZ) % NZ)
+            arrive(piece, base + stream * 4 + k - 1)
+            if k < hops:
+                send(piece, piece, z_peer(step), base + stream * 4 + k)
+
     def w_own(k):
-        piece = w_piece(xl, (z - k + NZ) % NZ)
-        arrive(piece, R_WRO + k - 1)
-        if k < 4:
-            send(piece, piece, right, R_WRO + k)
-            piece = w_piece(xl, (z + k) % NZ)
-            arrive(piece, R_WLO + k - 1)
-            if k < 3:
-                send(piece, piece, left, R_WLO + k)
+        w_step(0, k)
+        w_step(1, k)
 
     def w_par(k):
-        piece = w_piece(xo, (z + k) % NZ)
-        arrive(piece, R_WLP + k - 1)
-        if k < 4:
-            send(piece, piece, left, R_WLP + k)
-            piece = w_piece(xo, (z - k + NZ) % NZ)
-            arrive(piece, R_WRP + k - 1)
-            if k < 3:
-                send(piece, piece, right, R_WRP + k)
+        w_step(2, k)
+        w_step(3, k)
 
     w_local.wait()
     w_own(1)
-    arrive(w_piece(xo, z), R_WX)
-    send(w_piece(xo, z), w_piece(xo, z), left, R_WLP)
-    send(w_piece(xo, z), w_piece(xo, z), right, R_WRP)
+    for part in range(2):
+        arrive(w_piece(2 + part, z), R_WX + part)
+        w_start(2 + part, w_piece(2 + part, z))
     in_second(0)
 
     arrive(hn_v, R_H)

time: 68.3 us -> 66.8 us (0.978)
  Pallas kernels: 67.6 us -> 66 us
    pallas_call x1, Pallas kernels: 66.6 us -> 65 us  [body(): pl.pallas_call(kernel, out_shape=tuple((vmem(s.shape, s.dtype) for s in s...]
where the time goes in v3:
time: 66.8 us; the launch traced here: 66.7 us
  Pallas kernels  66 us (99%)
    pallas_call x1, Pallas kernels, body(): pl.pallas_call(kernel, out_shape=tuple((vmem(s.shape, s.dtype) for s in s...  65 us

profile of v3, /device:TPU:1, one launch (start us, length us, event | category | flops | bytes accessed | tf_op | source)
XLA Modules:
  0.0 66.7 jit_solution(6217802861866652169)
XLA Ops:
  0.6 65.0 %shard_map.119 = (bf16[128,1024]{1,0:T(8,128)(2,1)S(1)}, bf16[256,512]{1,0:T(8,128)(2,1)S(1)}, bf16[128,512]{1,0:T(8,128)(2,1)S(1)}, bf16[128,512]{1,0:T(8,128)(2,1)S(1)}, f32[128,512]{1,0:T(8,128)S(1)}) custom-call(bf16[128,1024]{1,0:T(8,128)(2,1)} %x_hbm.1, bf16[256,512]{1,0:T(8,128)(2,1)} %w_hbm.1, bf16[128,512]{1,0:T(8,128)(2,1)} %q_hbm.1, ...), custom_call_target="tpu_custom_call" | custom-call | flops 4294967296 | bytes 4194304 | tf_op jit(solution)/shard_map/pallas_call | solution.py:481
  65.7 1.0 %shard_map.120 = (bf16[128,1024]{1,0:T(8,128)(2,1)}, bf16[256,512]{1,0:T(8,128)(2,1)}, bf16[128,512]{1,0:T(8,128)(2,1)}, bf16[128,512]{1,0:T(8,128)(2,1)}, f32[128,512]{1,0:T(8,128)}) custom-call(bf16[128,1024]{1,0:T(8,128)(2,1)S(1)} %get-tuple-element.10.refs_0_, bf16[256,512]{1,0:T(8,128)(2,1)S(1)} %get-tuple-element.11.refs_1_, ...), custom_call_target="tpu_custom_call" | custom-call | tf_op jit(solution)/shard_map/pallas_call | solution.py:492

commit v4 on v3

--- a/solution.py
+++ b/solution.py
@@ -334,9 +334,6 @@
 
     ig_first(0)
     ig_first(1)
-    rs_step(3)
-    wx_s[...] = w_term(z, xo).astype(BF16)
-    send(wx_s, wx_r, partner, R_WG)
 
     arrive(val_c.at[0], R_VC)
     value = val_t[0, rows(core), :] + val_c[0].astype(F32)
@@ -360,7 +357,10 @@
         send(fq_s.at[xh_d * 2 + core_d], fq_r.at[place - 1], plane(d), R_F1 + place - 1)
     kg_v[...] = (gg_v[...] * value).astype(BF16)
     outs = [local(kg_v, kg_hbm)]
+    rs_step(3)
     rs_step(4)
+    wx_s[...] = w_term(z, xo).astype(BF16)
+    send(wx_s, wx_r, partner, R_WG)
 
     total = fg_v[:, lanes(tb)]
     for place in range(3):

time: 66.8 us -> 68 us (1.018)
  Pallas kernels: 66 us -> 67.3 us
    pallas_call x1, Pallas kernels: 65 us -> 66.3 us  [body(): pl.pallas_call(kernel, out_shape=tuple((vmem(s.shape, s.dtype) for s in s...]
where the time goes in v4:
time: 68 us; the launch traced here: 67.9 us
  Pallas kernels  67.3 us (99%)
    pallas_call x1, Pallas kernels, body(): pl.pallas_call(kernel, out_shape=tuple((vmem(s.shape, s.dtype) for s in s...  66.3 us

profile of v4, /device:TPU:1, one launch (start us, length us, event | category | flops | bytes accessed | tf_op | source)
XLA Modules:
  0.0 67.9 jit_solution(14997437534644334045)
XLA Ops:
  0.6 66.3 %shard_map.119 = (bf16[128,1024]{1,0:T(8,128)(2,1)S(1)}, bf16[256,512]{1,0:T(8,128)(2,1)S(1)}, bf16[128,512]{1,0:T(8,128)(2,1)S(1)}, bf16[128,512]{1,0:T(8,128)(2,1)S(1)}, f32[128,512]{1,0:T(8,128)S(1)}) custom-call(bf16[128,1024]{1,0:T(8,128)(2,1)} %x_hbm.1, bf16[256,512]{1,0:T(8,128)(2,1)} %w_hbm.1, bf16[128,512]{1,0:T(8,128)(2,1)} %q_hbm.1, ...), custom_call_target="tpu_custom_call" | custom-call | flops 4294967296 | bytes 4194304 | tf_op jit(solution)/shard_map/pallas_call | solution.py:481
  66.9 1.0 %shard_map.120 = (bf16[128,1024]{1,0:T(8,128)(2,1)}, bf16[256,512]{1,0:T(8,128)(2,1)}, bf16[128,512]{1,0:T(8,128)(2,1)}, bf16[128,512]{1,0:T(8,128)(2,1)}, f32[128,512]{1,0:T(8,128)}) custom-call(bf16[128,1024]{1,0:T(8,128)(2,1)S(1)} %get-tuple-element.10.refs_0_, bf16[256,512]{1,0:T(8,128)(2,1)S(1)} %get-tuple-element.11.refs_1_, ...), custom_call_target="tpu_custom_call" | custom-call | tf_op jit(solution)/shard_map/pallas_call | solution.py:492
